TPU v7x, 512 devices: a whole 4x8x8 slice. The times are simulated.
512 devices in a mesh: segment: 4 (over x), dp: 8 (over y), mp: 16 (over z, core).
Axes of the slice: x: 4, y: 8, z: 8, core: 2. Of those that a mesh axis runs over, the one named last changes fastest.
Arguments:
- pending_inputs: bfloat16 [4, 8192, 4096], P('segment', ('dp', 'mp')), may hold values from -6 to 6
- arriving_samples: bfloat16 [8192, 4096], P(('dp', 'mp')), may hold values from -6 to 6
- layer_rms_gain: float32 [4, 4096], P('segment'), may hold values from 0.25 to 1.75
- scorer_vectors: float32 [4, 4096], P('segment'), may hold values from -0.09375 to 0.09375
- gating_matrix: bfloat16 [4, 4096, 14336], P('segment', 'dp', 'mp'), may hold values from -0.09375 to 0.09375
- expansion_matrix: bfloat16 [4, 4096, 14336], P('segment', 'dp', 'mp'), may hold values from -0.09375 to 0.09375
- contraction_matrix: bfloat16 [4, 14336, 4096], P('segment', 'mp', 'dp'), may hold values from -0.046875 to 0.046875
- dispatch_lists: int32 [2, 4, 128, 8], P(None, 'segment', ('dp', 'mp')), may hold values from -1 to 63, as said below
Outputs:
- first_out: bfloat16 [4, 8192, 4096], P('segment', ('dp', 'mp'))
- second_out: bfloat16 [4, 8192, 4096], P('segment', ('dp', 'mp'))
Inputs may be any that keep to these rules, and one draw needn't show every extreme that they name: `dispatch_lists`: in each list of 8 slots the used slots come first and name distinct rows of the block; the other slots hold -1. Some block of every group of 8 blocks that share an mp index uses all 8 slots, and every such group (same tick and section) uses exactly 32 slots together.
All inputs are finite; a program needn't handle non-finite values.
Results may differ from a plain program's by a relative error of at most 0.0065.
Values may be sent and summed in bfloat16 or wider, within the bound.
No kernel may reach another device: no remote copies, remote signals or barrier semaphores. Data moves between devices by JAX's collectives and lax.ppermute only.
A program may use at most 64 MiB of HBM per device.

v0:
```python
import jax
import jax.numpy as jnp
from jax import lax
from jax.sharding import PartitionSpec as P


def from_behind(value, axis, steps):
    count = lax.axis_size(axis)
    initial, last = (max(0, -steps), min(count, count - steps))
    return lax.ppermute(value, axis, [(source, source + steps) for source in range(initial, last)])


def selection(flags, dense_rows):
    used_slots = (flags[:, 0] > 0).astype(jnp.int32)
    dense_place = jnp.cumsum(used_slots) - 1
    targets = jnp.arange(dense_rows, dtype=jnp.int32)[:, None]
    return ((dense_place[None, :] == targets) & (used_slots[None, :] > 0)).astype(jnp.bfloat16)


def layer_tile(section_in, route_row, gain, router_vec, w_gate_local, w_up_local, w_down_local):
    width_parts = lax.axis_size("dp")
    slot_count = route_row.shape[0]
    is_live = route_row >= 0
    safe_rows = jnp.where(is_live, route_row, 0)
    picked = jnp.take(section_in, safe_rows, axis=0)
    values = picked.astype(jnp.float32)
    inv_rms = lax.rsqrt(jnp.mean(values * values, axis=-1, keepdims=True) + 1e-05)
    normed = jnp.where(is_live[:, None], values * inv_rms * gain, 0.0).astype(jnp.bfloat16)
    live_flags = jnp.broadcast_to(is_live[:, None], (slot_count, width_parts)).astype(jnp.bfloat16)
    slot_rows, flag_col = (
        lax.all_to_all(normed, "dp", split_axis=1, concat_axis=0, tiled=True),
        lax.all_to_all(live_flags, "dp", split_axis=1, concat_axis=0, tiled=True),
    )
    group_rows = width_parts * slot_count // 2
    selector = selection(flag_col, group_rows)
    all_rows, all_flags = (
        lax.all_gather(slot_rows, "mp", axis=0, tiled=True),
        lax.all_gather(flag_col, "mp", axis=0, tiled=True),
    )
    wide_selector = selection(all_flags, lax.axis_size("mp") * group_rows)
    gathered = jnp.dot(wide_selector, all_rows, preferred_element_type=jnp.float32).astype(
        jnp.bfloat16
    )
    joined = jnp.concatenate([w_gate_local, w_up_local], axis=1)
    hidden_cols = w_gate_local.shape[1]
    summed = lax.psum_scatter(
        jnp.dot(gathered, joined, preferred_element_type=jnp.float32).astype(jnp.bfloat16),
        "dp",
        scatter_dimension=0,
        tiled=True,
    ).astype(jnp.float32)
    hidden = (jax.nn.silu(summed[:, :hidden_cols]) * summed[:, hidden_cols:]).astype(jnp.bfloat16)
    all_hidden = lax.all_gather(hidden, "dp", axis=0, tiled=True)
    partial_block = jnp.dot(all_hidden, w_down_local, preferred_element_type=jnp.float32)
    full_sum = lax.psum(partial_block.astype(jnp.bfloat16), "mp").astype(jnp.float32)
    block_out = lax.dynamic_slice_in_dim(full_sum, lax.axis_index("mp") * group_rows, group_rows, 0)
    block_out = block_out.astype(jnp.bfloat16)
    spread_out = jnp.dot(selector.T, block_out, preferred_element_type=jnp.float32).astype(
        jnp.bfloat16
    )
    returned = lax.all_to_all(spread_out, "dp", split_axis=0, concat_axis=1, tiled=True)
    weight = jax.nn.sigmoid(jnp.dot(values, router_vec, precision=lax.Precision.HIGHEST))
    updated = (values + weight[:, None] * returned.astype(jnp.float32)).astype(jnp.bfloat16)
    target = jnp.where(is_live, route_row, section_in.shape[0])
    return section_in.at[target].set(updated, mode="drop")


def local(
    pending_inputs,
    arriving_samples,
    layer_rms_gain,
    scorer_vectors,
    gating_matrix,
    expansion_matrix,
    contraction_matrix,
    dispatch_lists,
):
    first_local = layer_tile(
        pending_inputs[0],
        dispatch_lists[0, 0, 0],
        layer_rms_gain[0],
        scorer_vectors[0],
        gating_matrix[0],
        expansion_matrix[0],
        contraction_matrix[0],
    )
    passed = from_behind(first_local, "segment", 1)
    second_in = jnp.where(lax.axis_index("segment") == 0, arriving_samples, passed)
    second_local = layer_tile(
        second_in,
        dispatch_lists[1, 0, 0],
        layer_rms_gain[0],
        scorer_vectors[0],
        gating_matrix[0],
        expansion_matrix[0],
        contraction_matrix[0],
    )
    return (first_local[None], second_local[None])


def solution(mesh):
    return jax.shard_map(
        local,
        mesh=mesh,
        in_specs=(
            P("segment", ("dp", "mp"), None),
            P(("dp", "mp"), None),
            P("segment", None),
            P("segment", None),
            P("segment", "dp", "mp"),
            P("segment", "dp", "mp"),
            P("segment", "mp", "dp"),
            P(None, "segment", ("dp", "mp"), None),
        ),
        out_specs=(P("segment", ("dp", "mp"), None), P("segment", ("dp", "mp"), None)),
        check_vma=False,
    )
```

profile of v0, /device:TPU:2, one launch (start us, length us, event | category | flops | bytes accessed | tf_op | source)
XLA Modules:
  0.0 563.7 jit_solution(5471080146650865949)
XLA Ops:
  7.2 1.2 copy.25
  8.4 0.7 bitcast_compare_fusion
  9.1 0.6 gather_fusion
  9.7 0.2 fusion.34
  9.9 0.8 fusion.37
  10.7 15.4 %all_to_all.90 = bf16[8,8,512]{2,0,1:T(8,128)(2,1)} all-to-all(bf16[8,8,512]{2,0,1:T(8,128)(2,1)S(1)} %bitcast.119), channel_id=1, replica_groups=mesh['segment'=4,'dp'=8,'mp'=16] {'dp'}, dimensions={1} | all-to-all | bytes 131072 | tf_op jit(solution)/shard_map/all_to_all | solution.py:31
  26.1 0.6 broadcast_in_dim.43
  26.7 3.3 all-to-all-start
  30.1 1.3 dynamic-slice
  32.0 5.6 all-to-all-done
  37.6 0.6 broadcast_in_dim.77
  38.2 3.3 all-to-all-start.3
  41.6 0.1 reshape.343
  41.6 7.4 %all-to-all-done.3 = bf16[8,8,1]{0,2,1:T(2,128)(2,1)S(1)} async-done(((bf16[8,8,1]{0,2,1:T(2,128)(2,1)}), bf16[8,8,1]{0,2,1:T(2,128)(2,1)S(1)}, u32[]{:S(2)}, u32[]{:S(2)}) %all-to-all-start.3) | async-done | bytes 160 | tf_op jit(solution)/shard_map/all_to_all | solution.py:32
  49.0 0.1 reshape.346
  49.1 0.2 dynamic-update-slice
  49.4 0.2 dynamic-update-slice.1
  49.6 29.5 %all-reduce.2 = (bf16[1024]{0:T(1024)(128)(2,1)S(1)}, bf16[1024]{0:T(1024)(128)(2,1)S(1)}) all-reduce(bf16[1024]{0:T(1024)(128)(2,1)S(1)} %dynamic-update-slice, bf16[1024]{0:T(1024)(128)(2,1)S(1)} %dynamic-update-slice.1), channel_id=1, replica_groups=mesh['segment'=4,'dp'=8,'mp'=16] {'mp'}, use_global_device_ids=true, to_apply=%add | all-reduce | flops 2048 | bytes 8192
  79.0 0.3 reduce-window.39
  79.3 0.1 slice.33
  79.4 0.1 slice_reduce_fusion.1
  79.5 0.1 add_bitcast_fusion.1
  79.6 4.6 convolution_convert_fusion.1
  84.3 0.6 copy-done.7
  84.9 0.3 fusion.21
  85.2 37.5 %reduce-scatter.3.cloned.1.call-done = bf16[64,1792]{1,0:T(8,128)(2,1)} async-done(((bf16[512,1792]{1,0:T(8,128)(2,1)}), bf16[64,1792]{1,0:T(8,128)(2,1)}) %reduce-scatter.3.cloned.1.call-update) | async-done | bytes 229392 | tf_op jit(solution)/shard_map/reduce_scatter | solution.py:46
  122.8 1.0 convert_element_type.172
  123.7 0.1 fusion.33
  123.8 26.5 %all_gather.20 = bf16[512,896]{1,0:T(8,128)(2,1)S(1)} all-gather(bf16[64,896]{1,0:T(8,128)(2,1)S(1)} %fusion.33), channel_id=1, replica_groups=mesh['segment'=4,'dp'=8,'mp'=16] {'dp'}, dimensions={0}, use_global_device_ids=true | all-gather | bytes 1032192 | tf_op jit(solution)/shard_map/all_gather | solution.py:53
  150.3 1.5 convolution_convert_fusion.3
  151.9 0.1 gt.105
  152.1 0.1 reduce-window.38
  152.2 0.1 add_reduce_fusion.1
  152.3 114.6 %all-reduce.6.cloned.1.call-done = bf16[512,512]{1,0:T(8,128)(2,1)} async-done(((bf16[512,512]{1,0:T(8,128)(2,1)}), bf16[512,512]{1,0:T(8,128)(2,1)}) %all-reduce.6.cloned.1.call-update) | async-done | bytes 524304 | tf_op jit(solution)/shard_map/psum | solution.py:55
  266.9 1.6 fusion.12
  268.4 6.7 %all-to-all-start.2 = ((bf16[8,8,512]{2,1,0:T(8,128)(2,1)}), bf16[8,8,512]{2,1,0:T(8,128)(2,1)S(1)}, u32[]{:S(2)}, u32[]{:S(2)}) async-start(bf16[8,8,512]{2,1,0:T(8,128)(2,1)} %fusion.12), calls=%async_computation.3 | async-start | bytes 131072 | tf_op jit(solution)/shard_map/all_to_all | solution.py:61
  275.3 8.3 %all-to-all-done.2 = bf16[8,8,512]{2,1,0:T(8,128)(2,1)S(1)} async-done(((bf16[8,8,512]{2,1,0:T(8,128)(2,1)}), bf16[8,8,512]{2,1,0:T(8,128)(2,1)S(1)}, u32[]{:S(2)}, u32[]{:S(2)}) %all-to-all-start.2) | async-done | bytes 65568 | tf_op jit(solution)/shard_map/all_to_all | solution.py:61
  283.6 1.1 scatter_custom_fusion
  284.7 3.4 collective-permute-start
  288.1 10.7 %collective-permute-done = bf16[64,4096]{1,0:T(8,128)(2,1)S(1)} collective-permute-done((bf16[64,4096]{1,0:T(8,128)(2,1)S(1)}, bf16[64,4096]{1,0:T(8,128)(2,1)S(1)}, u32[]{:S(2)}, u32[]{:S(2)}) %collective-permute-start) | collective-permute-done | bytes 524320 | tf_op jit(solution)/shard_map/ppermute | solution.py:10
  298.9 0.6 gather_fusion.1
  299.5 0.2 fusion.39
  299.7 0.1 fusion.42
  299.8 11.4 %all_to_all.91 = bf16[8,8,512]{2,0,1:T(8,128)(2,1)} all-to-all(bf16[8,8,512]{2,0,1:T(8,128)(2,1)S(1)} %bitcast.120), channel_id=1, replica_groups=mesh['segment'=4,'dp'=8,'mp'=16] {'dp'}, dimensions={1} | all-to-all | bytes 131072 | tf_op jit(solution)/shard_map/all_to_all | solution.py:31
  311.3 0.3 reduce-window.42
  311.6 0.1 slice.38
  311.7 0.1 slice_reduce_fusion
  311.8 0.1 add_bitcast_fusion
  311.9 35.2 %all-gather.5.cloned.1.call-done = bf16[1024,512]{1,0:T(8,128)(2,1)} async-done(((bf16[64,512]{1,0:T(8,128)(2,1)}), bf16[1024,512]{1,0:T(8,128)(2,1)}) %all-gather.5.cloned.1.call-update) | async-done | bytes 1048592 | tf_op jit(solution)/shard_map/all_gather | solution.py:37
  347.0 4.9 convolution_convert_fusion
  352.0 42.1 %reduce-scatter.5.cloned.1.call-done = bf16[64,1792]{1,0:T(8,128)(2,1)} async-done(((bf16[512,1792]{1,0:T(8,128)(2,1)}), bf16[64,1792]{1,0:T(8,128)(2,1)}) %reduce-scatter.5.cloned.1.call-update) | async-done | bytes 229392 | tf_op jit(solution)/shard_map/reduce_scatter | solution.py:46
  394.1 1.0 convert_element_type.192
  395.2 26.3 %all_gather.23 = bf16[512,896]{1,0:T(8,128)(2,1)S(1)} all-gather(bf16[64,896]{1,0:T(8,128)(2,1)S(1)} %fusion.32), channel_id=1, replica_groups=mesh['segment'=4,'dp'=8,'mp'=16] {'dp'}, dimensions={0}, use_global_device_ids=true | all-gather | bytes 1032192 | tf_op jit(solution)/shard_map/all_gather | solution.py:53
  421.5 1.5 convolution_convert_fusion.2
  423.1 0.1 gt.112
  423.2 0.1 reduce-window.41
  423.3 0.1 add_reduce_fusion
  423.4 114.8 %all-reduce.8.cloned.1.call-done = bf16[512,512]{1,0:T(8,128)(2,1)} async-done(((bf16[512,512]{1,0:T(8,128)(2,1)}), bf16[512,512]{1,0:T(8,128)(2,1)}) %all-reduce.8.cloned.1.call-update) | async-done | bytes 524304 | tf_op jit(solution)/shard_map/psum | solution.py:55
  538.2 1.6 fusion.13
  539.8 6.7 %all-to-all-start.5 = ((bf16[8,8,512]{2,1,0:T(8,128)(2,1)}), bf16[8,8,512]{2,1,0:T(8,128)(2,1)S(1)}, u32[]{:S(2)}, u32[]{:S(2)}) async-start(bf16[8,8,512]{2,1,0:T(8,128)(2,1)} %fusion.13), calls=%async_computation.7 | async-start | bytes 131072 | tf_op jit(solution)/shard_map/all_to_all | solution.py:61
  546.6 0.3 fusion.17
  546.8 8.1 %all-to-all-done.5 = bf16[8,8,512]{2,1,0:T(8,128)(2,1)S(1)} async-done(((bf16[8,8,512]{2,1,0:T(8,128)(2,1)}), bf16[8,8,512]{2,1,0:T(8,128)(2,1)S(1)}, u32[]{:S(2)}, u32[]{:S(2)}) %all-to-all-start.5) | async-done | bytes 65568 | tf_op jit(solution)/shard_map/all_to_all | solution.py:61
  554.9 1.1 scatter_custom_fusion.1
  556.1 0.8 copy-done.2
  (49 shorter events, 0.9 us)
Async XLA Ops:
  7.2 143.1 %copy-start = (bf16[1,896,512]{2,1,0:T(8,128)(2,1)S(1)}, bf16[1,896,512]{2,1,0:T(8,128)(2,1)}, u32[]{:S(2)}) copy-start(bf16[1,896,512]{2,1,0:T(8,128)(2,1)} %param.16) | copy-start | bytes 2752516
  7.2 72.5 %copy-start.6 = (bf16[1,512,896]{2,1,0:T(8,128)(2,1)S(1)}, bf16[1,512,896]{2,1,0:T(8,128)(2,1)}, u32[]{:S(2)}) copy-start(bf16[1,512,896]{2,1,0:T(8,128)(2,1)} %param.15) | copy-start | bytes 2752516
  7.2 72.4 %all-gather.3.cloned.1.call-start = ((), (), s32[]{:S(2)}) async-start(), calls=%async_computation.8 | async-start | bytes 1114112 | tf_op jit(solution)/shard_map/all_gather | solution.py:37
  26.7 10.8 %all-to-all-start = ((bf16[8,8,1]{0,2,1:T(2,128)(2,1)}), bf16[8,8,1]{0,2,1:T(2,128)(2,1)S(1)}, u32[]{:S(2)}, u32[]{:S(2)}) async-start(bf16[8,8,1]{0,2,1:T(2,128)(2,1)} %broadcast_in_dim.43), calls=%async_computation | async-start | bytes 8192 | tf_op jit(solution)/shard_map/all_to_all | solution.py:32
  38.2 10.8 %all-to-all-start.3 = ((bf16[8,8,1]{0,2,1:T(2,128)(2,1)}), bf16[8,8,1]{0,2,1:T(2,128)(2,1)S(1)}, u32[]{:S(2)}, u32[]{:S(2)}) async-start(bf16[8,8,1]{0,2,1:T(2,128)(2,1)} %broadcast_in_dim.77), calls=%async_computation.4 | async-start | bytes 8192 | tf_op jit(solution)/shard_map/all_to_all | solution.py:32
  41.5 81.3 %reduce-scatter.3.cloned.1.call-start = ((), (), s32[]{:S(2)}) async-start(), calls=%async_computation.9 | async-start | bytes 2064384 | tf_op jit(solution)/shard_map/reduce_scatter | solution.py:46
  84.2 0.7 copy-start.7
  84.2 182.6 %all-reduce.6.cloned.1.call-start = ((), (), s32[]{:S(2)}) async-start(), calls=%async_computation.10 | async-start | bytes 1048576 | tf_op jit(solution)/shard_map/psum | solution.py:55
  150.3 125.0 %copy-start.5 = (s32[2,1,1,8]{3,2,1,0:T(1,128)S(1)}, s32[2,1,1,8]{3,2,1,0:T(1,128)}, u32[]{:S(2)}) copy-start(s32[2,1,1,8]{3,2,1,0:T(1,128)} %param.17) | copy-start | bytes 196
  150.3 148.5 %copy-start.3 = (bf16[64,4096]{1,0:T(8,128)(2,1)S(1)}, bf16[64,4096]{1,0:T(8,128)(2,1)}, u32[]{:S(2)}) copy-start(bf16[64,4096]{1,0:T(8,128)(2,1)} %param.11) | copy-start | bytes 1572868
  151.8 147.9 %copy-start.4 = (f32[1,4096]{1,0:T(1,128)S(1)}, f32[1,4096]{1,0:T(1,128)}, u32[]{:S(2)}) copy-start(f32[1,4096]{1,0:T(1,128)} %param.12) | copy-start | bytes 49156
  268.4 15.1 %all-to-all-start.2 = ((bf16[8,8,512]{2,1,0:T(8,128)(2,1)}), bf16[8,8,512]{2,1,0:T(8,128)(2,1)S(1)}, u32[]{:S(2)}, u32[]{:S(2)}) async-start(bf16[8,8,512]{2,1,0:T(8,128)(2,1)} %fusion.12), calls=%async_computation.3 | async-start | bytes 131072 | tf_op jit(solution)/shard_map/all_to_all | solution.py:61
  275.2 71.9 %all-gather.5.cloned.1.call-start = ((), (), s32[]{:S(2)}) async-start(), calls=%async_computation.11 | async-start | bytes 1114112 | tf_op jit(solution)/shard_map/all_gather | solution.py:37
  284.7 67.2 %copy-start.1 = (bf16[64,4096]{1,0:T(8,128)(2,1)}, bf16[64,4096]{1,0:T(8,128)(2,1)S(1)}, u32[]{:S(2)}) copy-start(bf16[64,4096]{1,0:T(8,128)(2,1)S(1)} %scatter_custom_fusion) | copy-start | bytes 1572868
  284.7 14.1 %collective-permute-start = (bf16[64,4096]{1,0:T(8,128)(2,1)S(1)}, bf16[64,4096]{1,0:T(8,128)(2,1)S(1)}, u32[]{:S(2)}, u32[]{:S(2)}) collective-permute-start(bf16[64,4096]{1,0:T(8,128)(2,1)S(1)} %scatter_custom_fusion), channel_id=1, source_target_pairs={{0,128},{128,256},{256,384},{1,129},{129,257},{257,385},{2,130},{1... | collective-permute-start | bytes 1572872 | tf_op jit(solution)/shard_map/ppermute | solution.py:10
  311.2 82.9 %reduce-scatter.5.cloned.1.call-start = ((), (), s32[]{:S(2)}) async-start(), calls=%async_computation.12 | async-start | bytes 2064384 | tf_op jit(solution)/shard_map/reduce_scatter | solution.py:46
  351.9 186.3 %all-reduce.8.cloned.1.call-start = ((), (), s32[]{:S(2)}) async-start(), calls=%async_computation.13 | async-start | bytes 1048576 | tf_op jit(solution)/shard_map/psum | solution.py:55
  539.8 15.1 %all-to-all-start.5 = ((bf16[8,8,512]{2,1,0:T(8,128)(2,1)}), bf16[8,8,512]{2,1,0:T(8,128)(2,1)S(1)}, u32[]{:S(2)}, u32[]{:S(2)}) async-start(bf16[8,8,512]{2,1,0:T(8,128)(2,1)} %fusion.13), calls=%async_computation.7 | async-start | bytes 131072 | tf_op jit(solution)/shard_map/all_to_all | solution.py:61
  556.0 0.8 copy-start.2
Sparse Core Ops, SparseCore 0:
  26.3 41.3 all-gather.2
  84.4 38.3 reduce-scatter.2
  151.9 114.8 all-reduce.5
  311.4 35.6 all-gather.4
  352.1 42.0 reduce-scatter.4
  423.2 115.0 all-reduce.7
where the time goes:
time: 565 us; the launch traced here: 564 us
  waiting for transfers between devices  384 us (68%)
  blocking collectives  109 us (19%)
  starting transfers between devices  23.7 us (4%)
  matrix products  16.2 us (3%)
  between operations  15 us (3%)
  other arithmetic  7.69 us (1%)
  local copies, waits for them, and re-layouts  7.64 us (1%)
    psum x2, waiting for transfers between devices, layer_tile(): lax.psum(partial_block.astype(jnp.bfloat16), 'mp').astype(jnp.float32)  229 us
    reduce_scatter x2, waiting for transfers between devices, layer_tile(): lax.psum_scatter(jnp.dot(gathered, joined, preferred_element_type=jnp.flo...  79.7 us
    all_gather x2, blocking collectives, layer_tile(): all_hidden = lax.all_gather(hidden, 'dp', axis=0, tiled=True)  52.8 us
    all_gather x2, waiting for transfers between devices, layer_tile(): lax.all_gather(slot_rows, 'mp', axis=0, tiled=True)  35.2 us
    unnamed x1, blocking collectives  29.5 us
    all_to_all x2, blocking collectives, layer_tile(): lax.all_to_all(normed, 'dp', split_axis=1, concat_axis=0, tiled=True)  26.8 us
    all_to_all x2, waiting for transfers between devices, layer_tile(): lax.all_to_all(spread_out, 'dp', split_axis=0, concat_axis=1, tiled=True)  16.4 us
    all_to_all x2, starting transfers between devices, layer_tile(): lax.all_to_all(spread_out, 'dp', split_axis=0, concat_axis=1, tiled=True)  13.5 us
  transfers between devices with their start and end apart: 11, of which 10 were waited for; matrix products, arithmetic and copies ran while one was open for 1% of the time, Pallas kernels for 0%

commit v1 on v0

--- a/solution.py
+++ b/solution.py
@@ -2,6 +2,27 @@
 import jax.numpy as jnp
 from jax import lax
 from jax.sharding import PartitionSpec as P
+
+
+def gather_around(array, axis, dim):
+    length, index, span = (lax.axis_size(axis), lax.axis_index(axis), array.shape[dim])
+    right = [(i, (i + 1) % length) for i in range(length)]
+    left = [(i, (i - 1) % length) for i in range(length)]
+    out = jnp.zeros((*array.shape[:dim], length * span, *array.shape[dim + 1 :]), array.dtype)
+    out = lax.dynamic_update_slice_in_dim(out, array, index * span, axis=dim)
+    from_left = from_right = array
+    middle = length // 2
+    for turn in range(1, middle + 1):
+        from_left = lax.ppermute(from_left, axis, right)
+        out = lax.dynamic_update_slice_in_dim(
+            out, from_left, (index - turn) % length * span, axis=dim
+        )
+        if turn < length - middle:
+            from_right = lax.ppermute(from_right, axis, left)
+            out = lax.dynamic_update_slice_in_dim(
+                out, from_right, (index + turn) % length * span, axis=dim
+            )
+    return out
 
 
 def from_behind(value, axis, steps):
@@ -34,7 +55,7 @@
     group_rows = width_parts * slot_count // 2
     selector = selection(flag_col, group_rows)
     all_rows, all_flags = (
-        lax.all_gather(slot_rows, "mp", axis=0, tiled=True),
+        gather_around(slot_rows, "mp", 0),
         lax.all_gather(flag_col, "mp", axis=0, tiled=True),
     )
     wide_selector = selection(all_flags, lax.axis_size("mp") * group_rows)

time: 565 us -> 596 us (1.055)
  starting transfers between devices: 23.7 us -> 75.6 us
  blocking collectives: 109 us -> 82.8 us
  waiting for transfers between devices: 384 us -> 390 us
    ppermute x0 -> x30, starting transfers between devices: none -> 41.5 us  [the longest x14 41.4 us: gather_around(): from_right = lax.ppermute(from_right, axis, left)]
    ppermute x0 -> x30, waiting for transfers between devices: none -> 36.3 us  [the longest x16 36.3 us: gather_around(): from_left = lax.ppermute(from_left, axis, right)]
    all_gather x2 -> x0, waiting for transfers between devices: 35.2 us -> none  [layer_tile(): lax.all_gather(slot_rows, 'mp', axis=0, tiled=True)]
    all_to_all x2 -> x0, blocking collectives: 26.8 us -> none  [layer_tile(): lax.all_to_all(normed, 'dp', split_axis=1, concat_axis=0, tiled=True)]
    all_to_all x0 -> x2, waiting for transfers between devices: none -> 8.17 us  [layer_tile(): lax.all_to_all(normed, 'dp', split_axis=1, concat_axis=0, tiled=True)]
    all_to_all x0 -> x2, starting transfers between devices: none -> 6.7 us  [layer_tile(): lax.all_to_all(normed, 'dp', split_axis=1, concat_axis=0, tiled=True)]
  transfers between devices with their start and end apart: 11 -> 41, of which waited for: 10 -> 26; matrix products, arithmetic and copies ran while one was open for 1% -> 1% of each run, Pallas kernels for 0% -> 0%
where the time goes in v1:
time: 596 us
  waiting for transfers between devices  390 us (65%)
  blocking collectives  82.8 us (14%)
  starting transfers between devices  75.6 us (13%)
  matrix products  15.9 us (3%)
  between operations  15 us (3%)
  other arithmetic  8.23 us (1%)
  local copies, waits for them, and re-layouts  8.11 us (1%)
    psum x2, waiting for transfers between devices, layer_tile(): lax.psum(partial_block.astype(jnp.bfloat16), 'mp').astype(jnp.float32)  230 us
    reduce_scatter x2, waiting for transfers between devices, layer_tile(): lax.psum_scatter(jnp.dot(gathered, joined, preferred_element_type=jnp.flo...  77.9 us
    all_gather x2, blocking collectives, layer_tile(): all_hidden = lax.all_gather(hidden, 'dp', axis=0, tiled=True)  52.7 us
    ppermute x14, starting transfers between devices, gather_around(): from_right = lax.ppermute(from_right, axis, left)  41.4 us
    ppermute x16, waiting for transfers between devices, gather_around(): from_left = lax.ppermute(from_left, axis, right)  36.3 us
    unnamed x1, blocking collectives  30 us
    all_to_all x2, waiting for transfers between devices, layer_tile(): lax.all_to_all(spread_out, 'dp', split_axis=0, concat_axis=1, tiled=True)  16.5 us
    all_to_all x2, starting transfers between devices, layer_tile(): lax.all_to_all(spread_out, 'dp', split_axis=0, concat_axis=1, tiled=True)  13.5 us
  transfers between devices with their start and end apart: 41, of which 26 were waited for; matrix products, arithmetic and copies ran while one was open for 1% of the time, Pallas kernels for 0%

profile of v1, /device:TPU:2, one launch (start us, length us, event | category | flops | bytes accessed | tf_op | source)
XLA Modules:
  0.0 595.6 jit_solution(4632991594485248005)
XLA Ops:
  7.2 1.1 copy.57
  9.6 7.1 %all-to-all-start = ((bf16[8,8,1]{0,2,1:T(2,128)(2,1)}), bf16[8,8,1]{0,2,1:T(2,128)(2,1)S(1)}, u32[]{:S(2)}, u32[]{:S(2)}) async-start(bf16[8,8,1]{0,2,1:T(2,128)(2,1)} %broadcast_in_dim.43), calls=%async_computation | async-start | bytes 8192 | tf_op jit(solution)/shard_map/all_to_all | solution.py:53
  18.3 1.3 dynamic-slice
  20.4 3.9 all-to-all-done
  24.9 3.3 all-to-all-start.3
  28.3 7.5 %all-to-all-done.3 = bf16[8,8,1]{0,2,1:T(2,128)(2,1)S(1)} async-done(((bf16[8,8,1]{0,2,1:T(2,128)(2,1)}), bf16[8,8,1]{0,2,1:T(2,128)(2,1)S(1)}, u32[]{:S(2)}, u32[]{:S(2)}) %all-to-all-start.3) | async-done | bytes 160 | tf_op jit(solution)/shard_map/all_to_all | solution.py:53
  35.8 3.4 all-to-all-start.1
  39.8 30.0 %all-reduce.2 = (bf16[1024]{0:T(1024)(128)(2,1)S(1)}, bf16[1024]{0:T(1024)(128)(2,1)S(1)}) all-reduce(bf16[1024]{0:T(1024)(128)(2,1)S(1)} %dynamic-update-slice, bf16[1024]{0:T(1024)(128)(2,1)S(1)} %dynamic-update-slice.1), channel_id=1, replica_groups=mesh['segment'=4,'dp'=8,'mp'=16] {'mp'}, use_global_device_ids=true, to_apply=%add | all-reduce | flops 2048 | bytes 8192
  70.4 3.0 collective-permute-start.1
  73.5 1.8 collective-permute-done
  75.3 3.0 collective-permute-start.3
  78.3 1.9 collective-permute-done.2
  80.2 3.0 collective-permute-start.5
  83.2 1.9 collective-permute-done.4
  85.1 3.0 collective-permute-start.7
  88.1 1.9 collective-permute-done.6
  90.0 3.0 collective-permute-start.9
  93.0 1.9 collective-permute-done.8
  94.9 3.0 collective-permute-start.11
  97.9 1.9 collective-permute-done.10
  99.8 3.0 collective-permute-start.13
  102.8 1.9 collective-permute-done.12
  104.8 4.9 collective-permute-done.14
  109.6 4.6 convolution_convert_fusion.1
  115.2 41.1 %reduce-scatter.3.cloned.1.call-done = bf16[64,1792]{1,0:T(8,128)(2,1)} async-done(((bf16[512,1792]{1,0:T(8,128)(2,1)}), bf16[64,1792]{1,0:T(8,128)(2,1)}) %reduce-scatter.3.cloned.1.call-update) | async-done | bytes 229392 | tf_op jit(solution)/shard_map/reduce_scatter | solution.py:67
  156.3 1.0 convert_element_type.172
  157.4 26.3 %all_gather.13 = bf16[512,896]{1,0:T(8,128)(2,1)S(1)} all-gather(bf16[64,896]{1,0:T(8,128)(2,1)S(1)} %fusion.33), channel_id=1, replica_groups=mesh['segment'=4,'dp'=8,'mp'=16] {'dp'}, dimensions={0}, use_global_device_ids=true | all-gather | bytes 1032192 | tf_op jit(solution)/shard_map/all_gather | solution.py:74
  183.7 1.5 convolution_convert_fusion.3
  185.7 114.7 %all-reduce.6.cloned.1.call-done = bf16[512,512]{1,0:T(8,128)(2,1)} async-done(((bf16[512,512]{1,0:T(8,128)(2,1)}), bf16[512,512]{1,0:T(8,128)(2,1)}) %all-reduce.6.cloned.1.call-update) | async-done | bytes 524304 | tf_op jit(solution)/shard_map/psum | solution.py:76
  300.4 1.6 fusion.12
  302.0 6.7 %all-to-all-start.2 = ((bf16[8,8,512]{2,1,0:T(8,128)(2,1)}), bf16[8,8,512]{2,1,0:T(8,128)(2,1)S(1)}, u32[]{:S(2)}, u32[]{:S(2)}) async-start(bf16[8,8,512]{2,1,0:T(8,128)(2,1)} %fusion.12), calls=%async_computation.3 | async-start | bytes 131072 | tf_op jit(solution)/shard_map/all_to_all | solution.py:82
  308.7 8.4 %all-to-all-done.2 = bf16[8,8,512]{2,1,0:T(8,128)(2,1)S(1)} async-done(((bf16[8,8,512]{2,1,0:T(8,128)(2,1)}), bf16[8,8,512]{2,1,0:T(8,128)(2,1)S(1)}, u32[]{:S(2)}, u32[]{:S(2)}) %all-to-all-start.2) | async-done | bytes 65568 | tf_op jit(solution)/shard_map/all_to_all | solution.py:82
  317.1 1.1 scatter_custom_fusion
  318.2 3.4 collective-permute-start.15
  322.1 10.2 %collective-permute-done.15 = bf16[64,4096]{1,0:T(8,128)(2,1)S(1)} collective-permute-done((bf16[64,4096]{1,0:T(8,128)(2,1)S(1)}, bf16[64,4096]{1,0:T(8,128)(2,1)S(1)}, u32[]{:S(2)}, u32[]{:S(2)}) %collective-permute-start.15) | collective-permute-done | bytes 524320 | tf_op jit(solution)/shard_map/ppermute | solution.py:31
  333.2 0.7 fusion.42
  333.9 3.4 all-to-all-start.4
  337.4 8.2 %all-to-all-done.4 = bf16[8,8,512]{2,0,1:T(8,128)(2,1)S(1)} async-done(((bf16[8,8,512]{2,0,1:T(8,128)(2,1)}), bf16[8,8,512]{2,0,1:T(8,128)(2,1)S(1)}, u32[]{:S(2)}, u32[]{:S(2)}) %all-to-all-start.4) | async-done | bytes 65568 | tf_op jit(solution)/shard_map/all_to_all | solution.py:52
  345.6 3.0 collective-permute-start.17
  348.6 1.8 collective-permute-done.16
  350.5 3.0 collective-permute-start.19
  353.5 1.9 collective-permute-done.18
  355.4 3.0 collective-permute-start.21
  358.4 1.9 collective-permute-done.20
  360.3 3.0 collective-permute-start.23
  363.3 1.9 collective-permute-done.22
  365.2 3.0 collective-permute-start.25
  368.2 1.9 collective-permute-done.24
  370.1 3.0 collective-permute-start.27
  373.1 1.9 collective-permute-done.26
  375.0 3.0 collective-permute-start.29
  378.0 1.9 collective-permute-done.28
  379.9 4.9 collective-permute-done.30
  384.8 4.6 convolution_convert_fusion
  389.4 36.8 %reduce-scatter.5.cloned.1.call-done = bf16[64,1792]{1,0:T(8,128)(2,1)} async-done(((bf16[512,1792]{1,0:T(8,128)(2,1)}), bf16[64,1792]{1,0:T(8,128)(2,1)}) %reduce-scatter.5.cloned.1.call-update) | async-done | bytes 229392 | tf_op jit(solution)/shard_map/reduce_scatter | solution.py:67
  426.2 1.0 convert_element_type.192
  427.3 26.4 %all_gather.15 = bf16[512,896]{1,0:T(8,128)(2,1)S(1)} all-gather(bf16[64,896]{1,0:T(8,128)(2,1)S(1)} %fusion.32), channel_id=1, replica_groups=mesh['segment'=4,'dp'=8,'mp'=16] {'dp'}, dimensions={0}, use_global_device_ids=true | all-gather | bytes 1032192 | tf_op jit(solution)/shard_map/all_gather | solution.py:74
  453.7 1.5 convolution_convert_fusion.2
  455.6 114.8 %all-reduce.8.cloned.1.call-done = bf16[512,512]{1,0:T(8,128)(2,1)} async-done(((bf16[512,512]{1,0:T(8,128)(2,1)}), bf16[512,512]{1,0:T(8,128)(2,1)}) %all-reduce.8.cloned.1.call-update) | async-done | bytes 524304 | tf_op jit(solution)/shard_map/psum | solution.py:76
  570.4 1.6 fusion.13
  572.0 6.7 %all-to-all-start.5 = ((bf16[8,8,512]{2,1,0:T(8,128)(2,1)}), bf16[8,8,512]{2,1,0:T(8,128)(2,1)S(1)}, u32[]{:S(2)}, u32[]{:S(2)}) async-start(bf16[8,8,512]{2,1,0:T(8,128)(2,1)} %fusion.13), calls=%async_computation.7 | async-start | bytes 131072 | tf_op jit(solution)/shard_map/all_to_all | solution.py:82
  579.0 8.1 %all-to-all-done.5 = bf16[8,8,512]{2,1,0:T(8,128)(2,1)S(1)} async-done(((bf16[8,8,512]{2,1,0:T(8,128)(2,1)}), bf16[8,8,512]{2,1,0:T(8,128)(2,1)S(1)}, u32[]{:S(2)}, u32[]{:S(2)}) %all-to-all-start.5) | async-done | bytes 65568 | tf_op jit(solution)/shard_map/all_to_all | solution.py:82
  587.1 1.1 scatter_custom_fusion.1
  588.2 0.8 copy-done.2
  (137 shorter events, 9.1 us)
Async XLA Ops:
  7.2 176.5 %copy-start = (bf16[1,896,512]{2,1,0:T(8,128)(2,1)S(1)}, bf16[1,896,512]{2,1,0:T(8,128)(2,1)}, u32[]{:S(2)}) copy-start(bf16[1,896,512]{2,1,0:T(8,128)(2,1)} %param.16) | copy-start | bytes 2752516
  7.2 10.4 %copy-start.4 = (f32[1,4096]{1,0:T(1,128)S(1)}, f32[1,4096]{1,0:T(1,128)}, u32[]{:S(2)}) copy-start(f32[1,4096]{1,0:T(1,128)} %param.12) | copy-start | bytes 49156
  9.6 14.7 %all-to-all-start = ((bf16[8,8,1]{0,2,1:T(2,128)(2,1)}), bf16[8,8,1]{0,2,1:T(2,128)(2,1)S(1)}, u32[]{:S(2)}, u32[]{:S(2)}) async-start(bf16[8,8,1]{0,2,1:T(2,128)(2,1)} %broadcast_in_dim.43), calls=%async_computation | async-start | bytes 8192 | tf_op jit(solution)/shard_map/all_to_all | solution.py:53
  24.9 10.9 %all-to-all-start.3 = ((bf16[8,8,1]{0,2,1:T(2,128)(2,1)}), bf16[8,8,1]{0,2,1:T(2,128)(2,1)S(1)}, u32[]{:S(2)}, u32[]{:S(2)}) async-start(bf16[8,8,1]{0,2,1:T(2,128)(2,1)} %broadcast_in_dim.77), calls=%async_computation.4 | async-start | bytes 8192 | tf_op jit(solution)/shard_map/all_to_all | solution.py:53
  35.8 34.6 %all-to-all-start.1 = ((bf16[8,8,512]{2,0,1:T(8,128)(2,1)}), bf16[8,8,512]{2,0,1:T(8,128)(2,1)S(1)}, u32[]{:S(2)}, u32[]{:S(2)}) async-start(bf16[8,8,512]{2,0,1:T(8,128)(2,1)} %bitcast.12), calls=%async_computation.1 | async-start | bytes 131072 | tf_op jit(solution)/shard_map/all_to_all | solution.py:52
  39.2 117.1 %reduce-scatter.3.cloned.1.call-start = ((), (), s32[]{:S(2)}) async-start(), calls=%async_computation.8 | async-start | bytes 2064384 | tf_op jit(solution)/shard_map/reduce_scatter | solution.py:67
  70.4 4.9 collective-permute-start
  70.4 4.9 collective-permute-start.1
  75.3 4.9 collective-permute-start.2
  75.3 4.9 collective-permute-start.3
  80.2 4.9 collective-permute-start.4
  80.2 4.9 collective-permute-start.5
  85.1 4.9 collective-permute-start.6
  85.1 4.9 collective-permute-start.7
  90.0 4.9 collective-permute-start.8
  90.0 4.9 collective-permute-start.9
  94.9 4.9 collective-permute-start.10
  94.9 4.9 collective-permute-start.11
  99.8 4.9 collective-permute-start.12
  99.8 4.9 collective-permute-start.13
  104.7 4.9 collective-permute-start.14
  114.2 0.7 copy-start.6
  114.2 186.1 %all-reduce.6.cloned.1.call-start = ((), (), s32[]{:S(2)}) async-start(), calls=%async_computation.9 | async-start | bytes 1048576 | tf_op jit(solution)/shard_map/psum | solution.py:76
  183.7 125.0 %copy-start.5 = (s32[2,1,1,8]{3,2,1,0:T(1,128)S(1)}, s32[2,1,1,8]{3,2,1,0:T(1,128)}, u32[]{:S(2)}) copy-start(s32[2,1,1,8]{3,2,1,0:T(1,128)} %param.17) | copy-start | bytes 196
  183.7 148.6 %copy-start.3 = (bf16[64,4096]{1,0:T(8,128)(2,1)S(1)}, bf16[64,4096]{1,0:T(8,128)(2,1)}, u32[]{:S(2)}) copy-start(bf16[64,4096]{1,0:T(8,128)(2,1)} %param.11) | copy-start | bytes 1572868
  302.0 15.1 %all-to-all-start.2 = ((bf16[8,8,512]{2,1,0:T(8,128)(2,1)}), bf16[8,8,512]{2,1,0:T(8,128)(2,1)S(1)}, u32[]{:S(2)}, u32[]{:S(2)}) async-start(bf16[8,8,512]{2,1,0:T(8,128)(2,1)} %fusion.12), calls=%async_computation.3 | async-start | bytes 131072 | tf_op jit(solution)/shard_map/all_to_all | solution.py:82
  318.2 30.4 %copy-start.1 = (bf16[64,4096]{1,0:T(8,128)(2,1)}, bf16[64,4096]{1,0:T(8,128)(2,1)S(1)}, u32[]{:S(2)}) copy-start(bf16[64,4096]{1,0:T(8,128)(2,1)S(1)} %scatter_custom_fusion) | copy-start | bytes 1572868
  318.2 14.1 %collective-permute-start.15 = (bf16[64,4096]{1,0:T(8,128)(2,1)S(1)}, bf16[64,4096]{1,0:T(8,128)(2,1)S(1)}, u32[]{:S(2)}, u32[]{:S(2)}) collective-permute-start(bf16[64,4096]{1,0:T(8,128)(2,1)S(1)} %scatter_custom_fusion), channel_id=1, source_target_pairs={{0,128},{128,256},{256,384},{1,129},{129,257},{257,385},{2,130},{1... | collective-permute-start | bytes 1572872 | tf_op jit(solution)/shard_map/ppermute | solution.py:31
  333.9 11.7 %all-to-all-start.4 = ((bf16[8,8,512]{2,0,1:T(8,128)(2,1)}), bf16[8,8,512]{2,0,1:T(8,128)(2,1)S(1)}, u32[]{:S(2)}, u32[]{:S(2)}) async-start(bf16[8,8,512]{2,0,1:T(8,128)(2,1)} %bitcast.31), calls=%async_computation.5 | async-start | bytes 131072 | tf_op jit(solution)/shard_map/all_to_all | solution.py:52
  337.3 88.9 %reduce-scatter.5.cloned.1.call-start = ((), (), s32[]{:S(2)}) async-start(), calls=%async_computation.10 | async-start | bytes 2064384 | tf_op jit(solution)/shard_map/reduce_scatter | solution.py:67
  345.6 4.9 collective-permute-start.16
  345.6 4.9 collective-permute-start.17
  350.5 4.9 collective-permute-start.18
  350.5 4.9 collective-permute-start.19
  355.4 4.9 collective-permute-start.20
  355.4 4.9 collective-permute-start.21
  360.3 4.9 collective-permute-start.22
  360.3 4.9 collective-permute-start.23
  365.2 4.9 collective-permute-start.24
  365.2 4.9 collective-permute-start.25
  370.1 4.9 collective-permute-start.26
  370.1 4.9 collective-permute-start.27
  375.0 4.9 collective-permute-start.28
  375.0 4.9 collective-permute-start.29
  379.9 4.9 collective-permute-start.30
  389.4 181.0 %all-reduce.8.cloned.1.call-start = ((), (), s32[]{:S(2)}) async-start(), calls=%async_computation.11 | async-start | bytes 1048576 | tf_op jit(solution)/shard_map/psum | solution.py:76
  572.0 15.1 %all-to-all-start.5 = ((bf16[8,8,512]{2,1,0:T(8,128)(2,1)}), bf16[8,8,512]{2,1,0:T(8,128)(2,1)S(1)}, u32[]{:S(2)}, u32[]{:S(2)}) async-start(bf16[8,8,512]{2,1,0:T(8,128)(2,1)} %fusion.13), calls=%async_computation.7 | async-start | bytes 131072 | tf_op jit(solution)/shard_map/all_to_all | solution.py:82
  588.2 0.8 copy-start.2
Sparse Core Ops, SparseCore 0:
  114.3 41.9 reduce-scatter.2
  185.3 114.9 all-reduce.5
  389.5 36.6 reduce-scatter.4
  455.3 115.0 all-reduce.7
